TPU v7x, 32 devices: a whole 2x2x4 slice. The times are simulated.
32 devices in a mesh: section: 4 (over x, core), tm: 4 (over z), space: 2 (over y).
Axes of the slice: x: 2, y: 2, z: 4, core: 2. Of those that a mesh axis runs over, the one named last changes fastest.
Arguments:
- video: bfloat16 [4, 8, 128, 1152], P('section', 'tm', 'space'), may hold values from -6 to 6
- conv_taps: float32 [4, 3, 1152], P('section'), may hold values from -3 to 3
- modulation: float32 [4, 6, 1152], P('section'), may hold values from -3 to 3
- w_qkv: bfloat16 [4, 1152, 3, 1152], P('section', None, None, 'space'), may hold values from -6 to 6
- w_out: bfloat16 [4, 1152, 1152], P('section', 'space'), may hold values from -0.1875 to 0.1875
- w_up: bfloat16 [4, 1152, 4608], P('section', None, 'space'), may hold values from -0.1875 to 0.1875
- w_down: bfloat16 [4, 4608, 1152], P('section', 'space'), may hold values from -0.09375 to 0.09375
Outputs:
- next_in: bfloat16 [4, 8, 128, 1152], P('section', 'tm', 'space')
All inputs are finite; a program needn't handle non-finite values.
Results may differ from a plain program's by a relative error of at most 0.013.
Values may be sent and summed in bfloat16 or wider, within the bound.
A program may use at most 64 MiB of HBM per device.

v0:
```python
import math

import jax
import jax.numpy as jnp
from jax import lax
from jax.sharding import PartitionSpec as P

D = 1152
HEADS = 16


def shifted(value, axis, steps):
    count = lax.axis_size(axis)
    initial, last = (max(0, -steps), min(count, count - steps))
    return lax.ppermute(value, axis, [(source, source + steps) for source in range(initial, last)])


def from_behind(block, axis, distance):
    devices = range(lax.axis_size(axis))
    route = [((i - distance) % len(devices), i) for i in devices]
    return lax.ppermute(block, axis, route)


def normalize(values_in):
    centre = jnp.mean(values_in, axis=-1, keepdims=True)
    variance = jnp.mean(jnp.square(values_in - centre), axis=-1, keepdims=True)
    return (values_in - centre) * lax.rsqrt(variance + 1e-06)


def modulated(values_in, shift_row, scale_row):
    return (normalize(values_in) * (1.0 + scale_row) + shift_row).astype(jnp.bfloat16)


def collect(rows_in):
    return lax.all_gather(rows_in, "space", axis=1, tiled=True)


def spread(terms):
    return lax.psum_scatter(
        terms.astype(jnp.bfloat16), "space", scatter_dimension=1, tiled=True
    ).astype(jnp.float32)


def attend(whole_rows, mod_table, query_w, out_w):
    head_size = D // HEADS
    attn_in = modulated(whole_rows.astype(jnp.float32), mod_table[0], mod_table[1])
    projected = jnp.einsum(
        "fte,ecn->ftcn", attn_in, query_w, preferred_element_type=jnp.float32
    ).astype(jnp.bfloat16)
    frames_here, tokens_all = (projected.shape[0], projected.shape[1])
    heads_here = projected.shape[3] // head_size
    projected = projected.reshape(frames_here, tokens_all, 3, heads_here, head_size)
    scores = jnp.einsum(
        "fqhe,fkhe->fhqk",
        projected[:, :, 0],
        projected[:, :, 1],
        preferred_element_type=jnp.float32,
    ) * (1.0 / math.sqrt(head_size))
    probs = jax.nn.softmax(scores, axis=-1).astype(jnp.bfloat16)
    heads_out = jnp.einsum(
        "fhqk,fkhe->fqhe", probs, projected[:, :, 2], preferred_element_type=jnp.float32
    ).astype(jnp.bfloat16)
    heads_out = heads_out.reshape(frames_here, tokens_all, heads_here * head_size)
    return jnp.einsum("ftk,kd->ftd", heads_out, out_w, preferred_element_type=jnp.float32)


def feed_forward(mlp_in, up_w, down_w):
    activated = jax.nn.gelu(
        jnp.einsum("fte,en->ftn", mlp_in, up_w, preferred_element_type=jnp.float32),
        approximate=True,
    ).astype(jnp.bfloat16)
    return jnp.einsum("ftn,nd->ftd", activated, down_w, preferred_element_type=jnp.float32)


def body(video, conv_taps, modulation, w_qkv, w_out, w_up, w_down):
    frames_in = video[0]
    tap_set = conv_taps[0]
    mod_table = modulation[0]
    earlier = shifted(frames_in, "tm", 1)
    extended = jnp.concatenate([earlier, frames_in], axis=0).astype(jnp.float32)
    mixed_rows = (
        extended[2:]
        + tap_set[0] * extended[2:]
        + tap_set[1] * extended[1:-1]
        + tap_set[2] * extended[:-2]
    ).astype(jnp.bfloat16)
    whole_rows = collect(mixed_rows)
    attn_part = attend(whole_rows, mod_table, w_qkv[0], w_out[0])
    hidden_state = mixed_rows.astype(jnp.float32) + mod_table[2] * spread(attn_part)
    mlp_whole = collect(modulated(hidden_state, mod_table[3], mod_table[4]))
    mlp_sum = spread(feed_forward(mlp_whole, w_up[0], w_down[0]))
    layer_out = (hidden_state + mod_table[5] * mlp_sum).astype(jnp.bfloat16)
    return from_behind(layer_out, "section", 1)[None]


def solution(mesh):
    placed = (
        P("section", "tm", "space", None),
        P("section", None, None),
        P("section", None, None),
        P("section", None, None, "space"),
        P("section", "space", None),
        P("section", None, "space"),
        P("section", "space", None),
    )
    return jax.shard_map(
        body,
        mesh=mesh,
        in_specs=placed,
        out_specs=P("section", "tm", "space", None),
        check_vma=False,
    )
```

profile of v0, /device:TPU:0, one launch (start us, length us, event | category | flops | bytes accessed | tf_op | source)
XLA Modules:
  0.0 106.1 jit_solution(1590679774460040285)
XLA Ops:
  6.5 0.0 copy-start
  6.5 0.0 reduce-scatter.3.cloned.1.call-start
  6.5 5.1 %collective-permute-start = (bf16[2,64,1152]{2,1,0:T(8,128)(2,1)}, bf16[2,64,1152]{2,1,0:T(8,128)(2,1)S(1)}, u32[]{:S(2)}, u32[]{:S(2)}) collective-permute-start(bf16[2,64,1152]{2,1,0:T(8,128)(2,1)} %bitcast.67), channel_id=1, source_target_pairs={{0,2},{2,4},{4,6},{1,3},{3,5},{5,7},{8,10},{10,12},{12,14},{9,11},... | collective-permute-start | bytes 884744 | tf_op jit(solution)/shard_map/ppermute | solution.py:15
  11.6 0.8 slice_reduce_fusion.6
  12.4 0.0 copy-start.3
  12.4 0.0 copy-start.5
  12.4 0.0 copy-start.7
  12.4 1.5 %slice_reduce_fusion.1 = (f32[1152]{0:T(1024)}, f32[1152]{0:T(1024)S(1)}, f32[1152]{0:T(1024)S(1)}, f32[1152]{0:T(1024)}, f32[1152]{0:T(1024)}, /*index=5*/f32[1152]{0:T(1024)}) fusion(f32[1,6,1152]{2,0,1:T(1,128)} %param.9), kind=kLoop, calls=%fused_computation.55 | loop fusion | flops 2304 | bytes 55296 | tf_op jit(solution)/shard_map/slice | solution.py:92
  13.9 4.3 %collective-permute-done = bf16[2,64,1152]{2,1,0:T(8,128)(2,1)S(1)} collective-permute-done((bf16[2,64,1152]{2,1,0:T(8,128)(2,1)}, bf16[2,64,1152]{2,1,0:T(8,128)(2,1)S(1)}, u32[]{:S(2)}, u32[]{:S(2)}) %collective-permute-start) | collective-permute-done | bytes 294944 | tf_op jit(solution)/shard_map/ppermute | solution.py:15
  18.2 1.0 maximum_convert_fusion
  19.2 0.0 copy-start.13
  19.2 0.1 fusion.38
  19.4 0.0 copy-done.3
  19.4 0.0 copy-done.5
  19.4 0.0 copy-done.7
  19.4 8.7 %all_gather.6 = bf16[2,128,1152]{2,1,0:T(8,128)(2,1)S(1)} all-gather(bf16[2,64,1152]{2,1,0:T(8,128)(2,1)S(1)} %fusion.38), channel_id=1, replica_groups=mesh['section'=4,'tm'=4,'space'=2] {'space'}, dimensions={1}, use_global_device_ids=true | all-gather | bytes 884736 | tf_op jit(solution)/shard_map/all_gather | solution.py:35
  28.1 0.2 convert_reduce_fusion
  28.2 0.3 fusion.30
  28.6 0.0 copy-done.13
  28.6 1.5 %fusion.23 = bf16[2,128,3,576]{1,3,2,0:T(8,128)(2,1)S(1)} fusion(bf16[1,1152,3,576]{1,3,2,0:T(8,128)(2,1)S(1)} %copy-done.13, bf16[2,128,1152]{2,1,0:T(8,128)(2,1)S(1)} %all_gather.6, f32[1152]{0:T(1024)S(1)} %get-tuple-element.6, f32[1152]{0:T(1024)S(1)} %get-tuple-element.7, f32[2,128]{1,0:T(2,128)S(1)} %add_rsqrt_fusion.1, ...), kind=kOutput, calls=%fused_computation.21 | convolution fusion | flops 1021427712 | bytes 5467136 | tf_op jit(solution)/shard_map/fte,ecn->ftcn/dot_general | solution.py:47
  30.0 0.0 copy-start.2
  30.1 0.9 copy-done.2
  31.0 1.1 %fusion.52 = f32[2,8,128]{2,1,0:T(8,128)} fusion(bf16[2,128,3,8,72]{1,4,3,2,0:T(8,128)(2,1)S(1)} %bitcast.63), kind=kOutput, calls=%fused_computation.72 | convolution fusion | flops 38535296 | bytes 598016 | tf_op jit(solution)/shard_map/sub | solution.py:59
  32.1 1.4 %convolution_multiply_fusion = f32[2,8,128,128]{2,3,1,0:T(8,128)S(1)} fusion(bf16[2,128,3,8,72]{1,4,3,2,0:T(8,128)(2,1)} %bitcast.64), kind=kOutput, calls=%fused_computation.25 | convolution fusion | flops 38010880 | bytes 1638400 | tf_op jit(solution)/shard_map/fqhe,fkhe->fhqk/dot_general | solution.py:53
  33.5 2.1 %convolution_convert_fusion.1 = bf16[2,8,72,128]{3,2,1,0:T(8,128)(2,1)} fusion(f32[2,8,128]{2,1,0:T(8,128)} %fusion.52, bf16[2,128,3,8,72]{1,4,3,2,0:T(8,128)(2,1)} %bitcast.65, f32[2,8,128,128]{2,3,1,0:T(8,128)S(1)} %convolution_multiply_fusion), kind=kOutput, calls=%fused_computation.27 | convolution fusion | flops 38684800 | bytes 2695168 | tf_op jit(solution)/shard_map/fhqk,fkhe->fqhe/dot_general | solution.py:60
  35.6 0.0 copy-done
  35.6 0.0 copy-start.4
  35.6 0.0 copy-start.6
  35.6 0.0 copy-start.8
  35.6 0.0 copy-start.9
  35.6 2.5 %convolution_convert_fusion = bf16[2,128,1152]{2,1,0:T(8,128)(2,1)} fusion(bf16[2,128,576]{1,2,0:T(8,128)(2,1)} %bitcast.66, bf16[1,576,1152]{2,1,0:T(8,128)(2,1)S(1)} %copy-done), kind=kOutput, calls=%fused_computation.8 | convolution fusion | flops 340033536 | bytes 2211840 | tf_op jit(solution)/shard_map/ftk,kd->ftd/dot_general | solution.py:64
  38.1 0.0 reduce-scatter.3.cloned.1.call-update
  38.1 0.0 reduce-scatter.5.cloned.1.call-start
  38.2 17.4 %reduce-scatter.3.cloned.1.call-done = bf16[2,64,1152]{2,1,0:T(8,128)(2,1)} async-done(((bf16[2,128,1152]{2,1,0:T(8,128)(2,1)}), bf16[2,64,1152]{2,1,0:T(8,128)(2,1)}) %reduce-scatter.3.cloned.1.call-update) | async-done | bytes 294928 | tf_op jit(solution)/shard_map/reduce_scatter | solution.py:39
  55.6 0.0 copy-start.1
  55.6 0.0 copy-done.4
  55.6 0.0 copy-done.6
  55.6 0.0 copy-done.8
  55.6 0.0 copy-done.9
  55.6 1.3 %fusion.45 = f32[2,64]{1,0:T(2,128)S(1)} fusion(bf16[2,64,1152]{2,1,0:T(8,128)(2,1)} %reduce-scatter.3.cloned.1.call-done, f32[1152]{0:T(1024)S(1)} %copy-done.9, f32[4,64,1152]{2,1,0:T(8,128)S(1)} %maximum_convert_fusion, f32[1152]{0:T(1024)S(1)} %copy-done.6, f32[1152]{0:T(1024)S(1)} %copy-done.8, f32[1152]{0:T(1024)S(1)} %copy-done.4), kind=kLoop, calls=%fused_computation.49 | loop fusion | flops 1769344 | bytes 2083328 | tf_op jit(solution)/shard_map/reduce_sum | solution.py:25
  56.9 0.0 copy-start.11
  56.9 0.0 copy-start.12
  56.9 0.0 copy-done.1
  56.9 0.3 multiply_reduce_fusion
  57.3 0.3 copy-done.11
  57.6 0.0 copy-done.12
  57.6 0.3 add_convert_fusion.1
  58.0 9.4 %all_gather.7 = bf16[2,128,1152]{2,1,0:T(8,128)(2,1)S(1)} all-gather(bf16[2,64,1152]{2,1,0:T(8,128)(2,1)S(1)} %add_convert_fusion.1), channel_id=1, replica_groups=mesh['section'=4,'tm'=4,'space'=2] {'space'}, dimensions={1}, use_global_device_ids=true | all-gather | bytes 884736 | tf_op jit(solution)/shard_map/all_gather | solution.py:35
  67.4 0.0 copy-start.10
  67.4 8.2 %fusion.7 = bf16[2,128,1152]{2,1,0:T(8,128)(2,1)} fusion(bf16[1,2304,1152]{2,1,0:T(8,128)(2,1)} %param.13, bf16[2,128,1152]{2,1,0:T(8,128)(2,1)S(1)} %all_gather.7, bf16[1,1152,2304]{2,1,0:T(8,128)(2,1)} %param.12), kind=kOutput, calls=%fused_computation.9 | convolution fusion | flops 2723512320 | bytes 11796480 | tf_op jit(solution)/shard_map/ftn,nd->ftd/dot_general | solution.py:72
  75.6 0.0 reduce-scatter.5.cloned.1.call-update
  75.7 15.4 %reduce-scatter.5.cloned.1.call-done = bf16[2,64,1152]{2,1,0:T(8,128)(2,1)} async-done(((bf16[2,128,1152]{2,1,0:T(8,128)(2,1)}), bf16[2,64,1152]{2,1,0:T(8,128)(2,1)}) %reduce-scatter.5.cloned.1.call-update) | async-done | bytes 294928 | tf_op jit(solution)/shard_map/reduce_scatter | solution.py:39
  91.1 0.0 copy-done.10
  91.1 1.2 %add_convert_fusion = bf16[2,64,1152]{2,1,0:T(8,128)(2,1)S(1)} fusion(bf16[2,64,1152]{2,1,0:T(8,128)(2,1)} %reduce-scatter.5.cloned.1.call-done, bf16[2,64,1152]{2,1,0:T(8,128)(2,1)S(1)} %copy-done.1, f32[1152]{0:T(1024)S(1)} %copy-done.10, f32[1152]{0:T(1024)S(1)} %copy-done.9, f32[4,64,1152]{2,1,0:T(8,128)S(1)} %maximum_convert_fusion, ...), kind=kLoop, calls=%fused_computation.41 | loop fusion | flops 2211840 | bytes 2677248 | tf_op jit(solution)/shard_map/convert_element_type | solution.py:92
  92.3 0.1 collective-permute-start.1
  92.4 6.1 %collective-permute-done.1 = bf16[2,64,1152]{2,1,0:T(8,128)(2,1)S(1)} collective-permute-done((bf16[2,64,1152]{2,1,0:T(8,128)(2,1)S(1)}, bf16[2,64,1152]{2,1,0:T(8,128)(2,1)S(1)}, u32[]{:S(2)}, u32[]{:S(2)}) %collective-permute-start.1) | collective-permute-done | bytes 294944 | tf_op jit(solution)/shard_map/ppermute | solution.py:21
  98.5 0.7 copy.18
  (4 shorter events, 0.0 us)
Async XLA Ops:
  6.5 29.0 %copy-start = (bf16[1,576,1152]{2,1,0:T(8,128)(2,1)S(1)}, bf16[1,576,1152]{2,1,0:T(8,128)(2,1)}, u32[]{:S(2)}) copy-start(bf16[1,576,1152]{2,1,0:T(8,128)(2,1)} %param.11) | copy-start | bytes 3981316
  6.5 49.1 %reduce-scatter.3.cloned.1.call-start = ((), (), s32[]{:S(2)}) async-start(), calls=%async_computation.2 | async-start | bytes 884736 | tf_op jit(solution)/shard_map/reduce_scatter | solution.py:39
  6.5 11.6 %collective-permute-start = (bf16[2,64,1152]{2,1,0:T(8,128)(2,1)}, bf16[2,64,1152]{2,1,0:T(8,128)(2,1)S(1)}, u32[]{:S(2)}, u32[]{:S(2)}) collective-permute-start(bf16[2,64,1152]{2,1,0:T(8,128)(2,1)} %bitcast.67), channel_id=1, source_target_pairs={{0,2},{2,4},{4,6},{1,3},{3,5},{5,7},{8,10},{10,12},{12,14},{9,11},... | collective-permute-start | bytes 884744 | tf_op jit(solution)/shard_map/ppermute | solution.py:15
  12.4 7.0 %copy-start.3 = (f32[1152]{0:T(1024)}, f32[1152]{0:T(1024)S(1)}, u32[]{:S(2)}) copy-start(f32[1152]{0:T(1024)S(1)} %get-tuple-element.11) | copy-start | bytes 13828
  12.4 7.0 %copy-start.5 = (f32[1152]{0:T(1024)}, f32[1152]{0:T(1024)S(1)}, u32[]{:S(2)}) copy-start(f32[1152]{0:T(1024)S(1)} %get-tuple-element.12) | copy-start | bytes 13828
  12.4 7.0 %copy-start.7 = (f32[1152]{0:T(1024)}, f32[1152]{0:T(1024)S(1)}, u32[]{:S(2)}) copy-start(f32[1152]{0:T(1024)S(1)} %get-tuple-element.13) | copy-start | bytes 13828
  19.2 9.4 %copy-start.13 = (bf16[1,1152,3,576]{1,3,2,0:T(8,128)(2,1)S(1)}, bf16[1,1152,3,576]{1,3,2,0:T(8,128)(2,1)}, u32[]{:S(2)}) copy-start(bf16[1,1152,3,576]{1,3,2,0:T(8,128)(2,1)} %param.10) | copy-start | bytes 11943940
  30.0 0.9 copy-start.2
  35.6 20.0 %copy-start.4 = (f32[1152]{0:T(1024)S(1)}, f32[1152]{0:T(1024)}, u32[]{:S(2)}) copy-start(f32[1152]{0:T(1024)} %copy-done.3) | copy-start | bytes 13828
  35.6 20.0 %copy-start.6 = (f32[1152]{0:T(1024)S(1)}, f32[1152]{0:T(1024)}, u32[]{:S(2)}) copy-start(f32[1152]{0:T(1024)} %copy-done.5) | copy-start | bytes 13828
  35.6 20.0 %copy-start.8 = (f32[1152]{0:T(1024)S(1)}, f32[1152]{0:T(1024)}, u32[]{:S(2)}) copy-start(f32[1152]{0:T(1024)} %copy-done.7) | copy-start | bytes 13828
  35.6 20.0 %copy-start.9 = (f32[1152]{0:T(1024)S(1)}, f32[1152]{0:T(1024)}, u32[]{:S(2)}) copy-start(f32[1152]{0:T(1024)} %get-tuple-element.8) | copy-start | bytes 13828
  38.1 53.0 %reduce-scatter.5.cloned.1.call-start = ((), (), s32[]{:S(2)}) async-start(), calls=%async_computation.3 | async-start | bytes 884736 | tf_op jit(solution)/shard_map/reduce_scatter | solution.py:39
  55.6 1.3 %copy-start.1 = (bf16[2,64,1152]{2,1,0:T(8,128)(2,1)S(1)}, bf16[2,64,1152]{2,1,0:T(8,128)(2,1)}, u32[]{:S(2)}) copy-start(bf16[2,64,1152]{2,1,0:T(8,128)(2,1)} %reduce-scatter.3.cloned.1.call-done) | copy-start | bytes 884740
  56.9 0.7 copy-start.11
  56.9 0.7 copy-start.12
  67.4 23.7 %copy-start.10 = (f32[1152]{0:T(1024)S(1)}, f32[1152]{0:T(1024)}, u32[]{:S(2)}) copy-start(f32[1152]{0:T(1024)} %get-tuple-element.5) | copy-start | bytes 13828
  92.3 6.2 %collective-permute-start.1 = (bf16[2,64,1152]{2,1,0:T(8,128)(2,1)S(1)}, bf16[2,64,1152]{2,1,0:T(8,128)(2,1)S(1)}, u32[]{:S(2)}, u32[]{:S(2)}) collective-permute-start(bf16[2,64,1152]{2,1,0:T(8,128)(2,1)S(1)} %add_convert_fusion), channel_id=1, source_target_pairs={{24,0},{0,8},{8,16},{16,24},{25,1},{1,9},{9,17},{17,25},{26,2},{2,... | collective-permute-start | bytes 884744 | tf_op jit(solution)/shard_map/ppermute | solution.py:21
Sparse Core Ops, SparseCore 0:
  38.2 17.3 reduce-scatter.2
  75.8 15.2 reduce-scatter.4
where the time goes:
time: 107 us; the launch traced here: 106 us
  waiting for transfers between devices  43.3 us (40%)
  blocking collectives  18.1 us (17%)
  matrix products  16.8 us (16%)
  between operations  13.6 us (13%)
  other arithmetic  6.28 us (6%)
  starting transfers between devices  5.17 us (5%)
  local copies, waits for them, and re-layouts  2.8 us (3%)
    reduce_scatter x2, waiting for transfers between devices, spread(): lax.psum_scatter(terms.astype(jnp.bfloat16), 'space', scatter_dimension=1...  32.9 us
    all_gather x2, blocking collectives, collect(): return lax.all_gather(rows_in, 'space', axis=1, tiled=True)  18.1 us
    dot_general x1, matrix products, feed_forward(): jnp.einsum('ftn,nd->ftd', activated, down_w, preferred_element_type=jnp.f...  8.24 us
    ppermute x1, waiting for transfers between devices, from_behind(): return lax.ppermute(block, axis, route)  6.13 us
    ppermute x1, starting transfers between devices, shifted(): lax.ppermute(value, axis, [(source, source + steps) for source in range(i...  5.07 us
    ppermute x1, waiting for transfers between devices, shifted(): lax.ppermute(value, axis, [(source, source + steps) for source in range(i...  4.3 us
    dot_general x1, matrix products, attend(): jnp.einsum('ftk,kd->ftd', heads_out, out_w, preferred_element_type=jnp.fl...  2.5 us
  transfers between devices with their start and end apart: 4, of which 4 were waited for; matrix products, arithmetic and copies ran while one was open for 2% of the time, Pallas kernels for 0%

commit v1 on v0

v1 whole, which is shorter than its diff:
```python
import functools
import math

import jax
import jax.numpy as jnp
from jax import lax
from jax.experimental import pallas as pl
from jax.experimental.pallas import tpu as pltpu
from jax.sharding import PartitionSpec as P

D = 1152
HEADS = 16
MESH = pl.DeviceIdType.MESH


def normalize(values_in):
    centre = jnp.mean(values_in, axis=-1, keepdims=True)
    variance = jnp.mean(jnp.square(values_in - centre), axis=-1, keepdims=True)
    return (values_in - centre) * lax.rsqrt(variance + 1e-06)


def modulated(values_in, shift_row, scale_row):
    return (normalize(values_in) * (1.0 + scale_row) + shift_row).astype(jnp.bfloat16)


def dot(a, b, dims=((1,), (0,))):
    return lax.dot_general(a, b, (dims, ((), ())), preferred_element_type=jnp.float32)


def chunks(total, size):
    size = size if total % size == 0 else total
    return [(start, size) for start in range(0, total, size)]


def layer(
    sizes, video, taps, mod, qkv_hbm, out_hbm, up_hbm, down_hbm, result,
    frames, halo, mixed, part, part_in, hidden, heads, active, term, term_in, final,
    qkv_w, out_w, up_w, down_w,
    local_sem, halo_send, halo_recv, mix_send, mix_recv, part_send, part_recv,
    term_send, term_recv, end_send, end_recv,
):
    n_section, n_tm, n_space = sizes
    n_frames, tokens, width = frames.shape
    row = n_space * tokens
    section = lax.axis_index("section")
    tm = lax.axis_index("tm")
    me = lax.axis_index("space")
    after = lax.rem(section + 1, n_section)
    before = lax.rem(section + n_section - 1, n_section)
    peers = [lax.rem(me + j, n_space) for j in range(1, n_space)]
    order = list(range(n_frames - 1, -1, -1))

    video_copy = pltpu.make_async_copy(video.at[0], frames, local_sem.at[0])
    video_copy.start()
    weights = [
        pltpu.make_async_copy(source.at[0], target, local_sem.at[1 + i])
        for i, (source, target) in enumerate(
            ((qkv_hbm, qkv_w), (out_hbm, out_w), (up_hbm, up_w), (down_hbm, down_w))
        )
    ]
    for copy in weights:
        copy.start()

    barrier = pltpu.get_barrier_semaphore()
    for peer in peers:
        pl.semaphore_signal(barrier, inc=1, device_id={"space": peer}, device_id_type=MESH)
    for neighbour in (before, after):
        pl.semaphore_signal(barrier, inc=1, device_id={"section": neighbour}, device_id_type=MESH)

    @pl.when(tm > 0)
    def _():
        pl.semaphore_signal(barrier, inc=1, device_id={"tm": tm - 1}, device_id_type=MESH)

    @pl.when(tm < n_tm - 1)
    def _():
        pl.semaphore_signal(barrier, inc=1, device_id={"tm": tm + 1}, device_id_type=MESH)

    along_tm = lax.div(tm + n_tm - 1, n_tm) + 1 - lax.div(tm + 1, n_tm)
    pl.semaphore_wait(barrier, n_space + 1 + along_tm)

    halo_copies = [
        pltpu.make_async_remote_copy(
            src_ref=video.at[0, n_frames - 2 + i],
            dst_ref=halo.at[i],
            send_sem=halo_send.at[i],
            recv_sem=halo_recv.at[i],
            device_id={"tm": lax.rem(tm + 1, n_tm)},
            device_id_type=MESH,
        )
        for i in range(2)
    ]

    @pl.when(tm < n_tm - 1)
    def _():
        halo_copies[1].start()
        halo_copies[0].start()

    @pl.when(tm == 0)
    def _():
        halo[...] = jnp.zeros_like(halo)

    video_copy.wait()

    mix_copies = {}
    arrived = set()
    for f in order:
        terms = []
        for step in range(3):
            at = f - step
            if at >= 0:
                terms.append(frames[at])
            else:
                slot = at + 2
                if slot not in arrived:
                    arrived.add(slot)

                    @pl.when(tm > 0)
                    def _():
                        halo_copies[slot].wait_recv()

                terms.append(halo[slot])
        current, previous, second = (t.astype(jnp.float32) for t in terms)
        mixed[f, me] = (
            current + taps[0] * current + taps[1] * previous + taps[2] * second
        ).astype(jnp.bfloat16)
        for j, peer in enumerate(peers):
            mix_copies[f, j] = pltpu.make_async_remote_copy(
                src_ref=mixed.at[f, me],
                dst_ref=mixed.at[f, me],
                send_sem=mix_send.at[f, j],
                recv_sem=mix_recv.at[f, j],
                device_id={"space": peer},
                device_id_type=MESH,
            )
            mix_copies[f, j].start()

    part_copies = {}
    head_size = D // HEADS
    scale = 1.0 / math.sqrt(head_size)
    for position, f in enumerate(order):
        for j in range(len(peers)):
            mix_copies[f, j].wait_recv()
        rows = mixed[f].reshape(row, width).astype(jnp.float32)
        attn_in = modulated(rows, mod[0], mod[1])
        if position == 0:
            weights[0].wait()
        queries, keys, values = (dot(qkv_w[c], attn_in, ((1,), (1,))) for c in range(3))
        for h in range(queries.shape[0] // head_size):
            span = slice(h * head_size, (h + 1) * head_size)
            key_rows = keys[span].T.astype(jnp.bfloat16)
            scores = dot(key_rows, queries[span].astype(jnp.bfloat16)) * scale
            shifted = jnp.exp(scores - jnp.max(scores, axis=0, keepdims=True))
            probs = shifted / jnp.sum(shifted, axis=0, keepdims=True)
            heads[span] = dot(values[span].astype(jnp.bfloat16), probs.astype(jnp.bfloat16))
        heads_out = heads[...].T.astype(jnp.bfloat16)
        if position == 0:
            weights[1].wait()
        for start, size in chunks(width, 384):
            part[f, :, start : start + size] = dot(
                heads_out, out_w[:, start : start + size]
            ).astype(jnp.bfloat16)
        for j, peer in enumerate(peers):
            part_copies[f, j] = pltpu.make_async_remote_copy(
                src_ref=part.at[f],
                dst_ref=part_in.at[f, j],
                send_sem=part_send.at[f, j],
                recv_sem=part_recv.at[f, j],
                device_id={"space": peer},
                device_id_type=MESH,
            )
            part_copies[f, j].start()

    term_copies = {}
    for position, f in enumerate(order):
        for j in range(len(peers)):
            part_copies[f, j].wait_recv()
        attn_sum = part[f].astype(jnp.float32)
        for j in range(len(peers)):
            attn_sum = attn_sum + part_in[f, j].astype(jnp.float32)
        state = mixed[f].reshape(row, width).astype(jnp.float32) + mod[2] * attn_sum
        hidden[f] = state.reshape(n_space, tokens, width)
        mlp_in = modulated(state, mod[3], mod[4])
        if position == 0:
            weights[2].wait()
        for start, size in chunks(up_w.shape[1], 768):
            active[:, start : start + size] = jax.nn.gelu(
                dot(mlp_in, up_w[:, start : start + size]), approximate=True
            ).astype(jnp.bfloat16)
        if position == 0:
            weights[3].wait()
        for start, size in chunks(width, 384):
            term[f, :, :, start : start + size] = (
                dot(active[...], down_w[:, start : start + size])
                .astype(jnp.bfloat16)
                .reshape(n_space, tokens, size)
            )
        for j, peer in enumerate(peers):
            term_copies[f, j] = pltpu.make_async_remote_copy(
                src_ref=term.at[f, peer],
                dst_ref=term_in.at[f, j],
                send_sem=term_send.at[f, j],
                recv_sem=term_recv.at[f, j],
                device_id={"space": peer},
                device_id_type=MESH,
            )
            term_copies[f, j].start()

    end_copies = []
    for f in order:
        for j in range(len(peers)):
            term_copies[f, j].wait_recv()
        mlp_sum = term[f, me].astype(jnp.float32)
        for j in range(len(peers)):
            mlp_sum = mlp_sum + term_in[f, j].astype(jnp.float32)
        final[f] = (hidden[f, me] + mod[5] * mlp_sum).astype(jnp.bfloat16)
        copy = pltpu.make_async_remote_copy(
            src_ref=final.at[f],
            dst_ref=result.at[0, f],
            send_sem=end_send.at[f],
            recv_sem=end_recv.at[f],
            device_id={"section": after},
            device_id_type=MESH,
        )
        copy.start()
        end_copies.append(copy)

    @pl.when(tm < n_tm - 1)
    def _():
        for copy in halo_copies:
            copy.wait_send()

    for group in (mix_copies, part_copies, term_copies):
        for copy in group.values():
            copy.wait_send()
    for copy in end_copies:
        copy.wait()


def body(sizes, video, conv_taps, modulation, w_qkv, w_out, w_up, w_down):
    n_space = sizes[2]
    _, n_frames, tokens, width = video.shape
    row = n_space * tokens
    columns = w_qkv.shape[3]
    units = w_up.shape[2]
    bf16, f32 = jnp.bfloat16, jnp.float32
    others = max(n_space - 1, 1)
    sem = pltpu.SemaphoreType.DMA
    anywhere = pl.BlockSpec(memory_space=pl.ANY)
    vmem = pl.BlockSpec(memory_space=pltpu.VMEM)
    total = n_frames * row
    return pl.pallas_call(
        functools.partial(layer, sizes),
        out_shape=jax.ShapeDtypeStruct(video.shape, bf16),
        in_specs=[anywhere, vmem, vmem, anywhere, anywhere, anywhere, anywhere],
        out_specs=anywhere,
        scratch_shapes=[
            pltpu.VMEM((n_frames, tokens, width), bf16),
            pltpu.VMEM((2, tokens, width), bf16),
            pltpu.VMEM((n_frames, n_space, tokens, width), bf16),
            pltpu.VMEM((n_frames, row, width), bf16),
            pltpu.VMEM((n_frames, others, row, width), bf16),
            pltpu.VMEM((n_frames, n_space, tokens, width), f32),
            pltpu.VMEM((columns, row), f32),
            pltpu.VMEM((row, units), bf16),
            pltpu.VMEM((n_frames, n_space, tokens, width), bf16),
            pltpu.VMEM((n_frames, others, tokens, width), bf16),
            pltpu.VMEM((n_frames, tokens, width), bf16),
            pltpu.VMEM((3, columns, width), bf16),
            pltpu.VMEM((columns, width), bf16),
            pltpu.VMEM((width, units), bf16),
            pltpu.VMEM((units, width), bf16),
            sem((5,)),
            sem((2,)),
            sem((2,)),
            sem((n_frames, others)),
            sem((n_frames, others)),
            sem((n_frames, others)),
            sem((n_frames, others)),
            sem((n_frames, others)),
            sem((n_frames, others)),
            sem((n_frames,)),
            sem((n_frames,)),
        ],
        compiler_params=pltpu.CompilerParams(
            collective_id=0, has_side_effects=True, vmem_limit_bytes=56 * 1024 * 1024
        ),
        cost_estimate=pl.CostEstimate(
            flops=2 * total * width * (4 * columns + 2 * units),
            bytes_accessed=2 * width * (4 * columns + 2 * units),
            transcendentals=total * units,
        ),
    )(
        video,
        jnp.transpose(conv_taps, (1, 0, 2)),
        jnp.transpose(modulation, (1, 0, 2)),
        jnp.transpose(w_qkv, (0, 2, 3, 1)),
        w_out,
        w_up,
        w_down,
    )


def solution(mesh):
    sizes = (mesh.shape["section"], mesh.shape["tm"], mesh.shape["space"])
    placed = (
        P("section", "tm", "space", None),
        P("section", None, None),
        P("section", None, None),
        P("section", None, None, "space"),
        P("section", "space", None),
        P("section", None, "space"),
        P("section", "space", None),
    )
    return jax.shard_map(
        functools.partial(body, sizes),
        mesh=mesh,
        in_specs=placed,
        out_specs=P("section", "tm", "space", None),
        check_vma=False,
    )
```

time: 107 us -> 42.5 us (0.40)
  the two profiles are of different devices: /device:TPU:0 before, /device:TPU:19 now
where the time goes in v1:
time: 42.5 us; the launch traced here: 42.2 us
  Pallas kernels  40.5 us (95%)
  local copies, waits for them, and re-layouts  1.7 us (4%)
    pallas_call x1, Pallas kernels, body(): pl.pallas_call(functools.partial(layer, sizes), out_shape=jax.ShapeDtypeS...  40.5 us
    unnamed x1, local copies, waits for them, and re-layouts  1.7 us

profile of v1, /device:TPU:19, one launch (start us, length us, event | category | flops | bytes accessed | tf_op | source)
XLA Modules:
  0.0 42.2 jit_solution(8091510466235141513)
XLA Ops:
  0.0 40.5 %shard_map.73 = bf16[1,2,64,1152]{3,2,1,0:T(8,128)(2,1)} custom-call(bf16[1,2,64,1152]{3,2,1,0:T(8,128)(2,1)} %video.1, f32[3,1,1152]{2,1,0:T(1,128)} %bitcast.5, f32[6,1,1152]{2,1,0:T(1,128)} %bitcast.4, bf16[1,3,576,1152]{3,2,1,0:T(8,128)(2,1)} %bitcast.3, bf16[1,576,1152]{2,1,0:T(8,128)(2,1)} %out_hbm.1, bf16[1,1152,2304]{2,1,0:T(8,128)(2,1)} %up_hbm.1, ...), custom_call_target="tpu_custom_call" | custom-call | flops 4076863488 | bytes 15925248 | tf_op jit(solution)/shard_map/pallas_call | solution.py:251
  40.5 1.7 %copy.9 = bf16[1,2,64,1152]{3,2,1,0:T(8,128)(2,1)} copy(bf16[1,2,64,1152]{3,2,1,0:T(8,128)(2,1)} %shard_map.73) | data formatting | bytes 589824

commit v2 on v1

--- a/solution.py
+++ b/solution.py
@@ -11,6 +11,8 @@
 D = 1152
 HEADS = 16
 MESH = pl.DeviceIdType.MESH
+PIECES = 4
+SPAN = 384
 
 
 def normalize(values_in):
@@ -30,6 +32,11 @@
 def chunks(total, size):
     size = size if total % size == 0 else total
     return [(start, size) for start in range(0, total, size)]
+
+
+def row_pieces(tokens):
+    count = PIECES if tokens % (16 * PIECES) == 0 else 1
+    return [(i * (tokens // count), tokens // count) for i in range(count)]
 
 
 def layer(
@@ -58,8 +65,7 @@
             ((qkv_hbm, qkv_w), (out_hbm, out_w), (up_hbm, up_w), (down_hbm, down_w))
         )
     ]
-    for copy in weights:
-        copy.start()
+    weights[0].start()
 
     barrier = pltpu.get_barrier_semaphore()
     for peer in peers:
@@ -78,68 +84,76 @@
     along_tm = lax.div(tm + n_tm - 1, n_tm) + 1 - lax.div(tm + 1, n_tm)
     pl.semaphore_wait(barrier, n_space + 1 + along_tm)
 
-    halo_copies = [
-        pltpu.make_async_remote_copy(
-            src_ref=video.at[0, n_frames - 2 + i],
-            dst_ref=halo.at[i],
-            send_sem=halo_send.at[i],
-            recv_sem=halo_recv.at[i],
+    video_copy.wait()
+    pieces = row_pieces(tokens)
+    halo_copies = {
+        (i, p): pltpu.make_async_remote_copy(
+            src_ref=frames.at[n_frames - 2 + i, pl.ds(start, size)],
+            dst_ref=halo.at[i, pl.ds(start, size)],
+            send_sem=halo_send.at[i, p],
+            recv_sem=halo_recv.at[i, p],
             device_id={"tm": lax.rem(tm + 1, n_tm)},
             device_id_type=MESH,
         )
-        for i in range(2)
-    ]
+        for i in (1, 0)
+        for p, (start, size) in enumerate(pieces)
+    }
 
     @pl.when(tm < n_tm - 1)
     def _():
-        halo_copies[1].start()
-        halo_copies[0].start()
+        for copy in halo_copies.values():
+            copy.start()
 
     @pl.when(tm == 0)
     def _():
         halo[...] = jnp.zeros_like(halo)
 
-    video_copy.wait()
+    for copy in weights[1:]:
+        copy.start()
 
     mix_copies = {}
     arrived = set()
     for f in order:
-        terms = []
-        for step in range(3):
-            at = f - step
-            if at >= 0:
-                terms.append(frames[at])
-            else:
-                slot = at + 2
-                if slot not in arrived:
-                    arrived.add(slot)
-
-                    @pl.when(tm > 0)
-                    def _():
-                        halo_copies[slot].wait_recv()
-
-                terms.append(halo[slot])
-        current, previous, second = (t.astype(jnp.float32) for t in terms)
-        mixed[f, me] = (
-            current + taps[0] * current + taps[1] * previous + taps[2] * second
-        ).astype(jnp.bfloat16)
-        for j, peer in enumerate(peers):
-            mix_copies[f, j] = pltpu.make_async_remote_copy(
-                src_ref=mixed.at[f, me],
-                dst_ref=mixed.at[f, me],
-                send_sem=mix_send.at[f, j],
-                recv_sem=mix_recv.at[f, j],
-                device_id={"space": peer},
-                device_id_type=MESH,
-            )
-            mix_copies[f, j].start()
+        for p, (start, size) in enumerate(pieces):
+            rows = slice(start, start + size)
+            terms = []
+            for step in range(3):
+                at = f - step
+                if at >= 0:
+                    terms.append(frames[at, rows])
+                else:
+                    slot = at + 2
+                    if (slot, p) not in arrived:
+                        arrived.add((slot, p))
+
+                        @pl.when(tm > 0)
+                        def _():
+                            halo_copies[slot, p].wait_recv()
+
+                    terms.append(halo[slot, rows])
+            current, previous, second = (t.astype(jnp.float32) for t in terms)
+            mixed[f, me, rows] = (
+                current + taps[0] * current + taps[1] * previous + taps[2] * second
+            ).astype(jnp.bfloat16)
+            for j, peer in enumerate(peers):
+                mix_copies[f, j, p] = pltpu.make_async_remote_copy(
+                    src_ref=mixed.at[f, me, pl.ds(start, size)],
+                    dst_ref=mixed.at[f, me, pl.ds(start, size)],
+                    send_sem=mix_send.at[f, j, p],
+                    recv_sem=mix_recv.at[f, j, p],
+                    device_id={"space": peer},
+                    device_id_type=MESH,
+                )
+                mix_copies[f, j, p].start()
 
     part_copies = {}
+    spans = chunks(width, SPAN)
     head_size = D // HEADS
     scale = 1.0 / math.sqrt(head_size)
     for position, f in enumerate(order):
         for j in range(len(peers)):
-            mix_copies[f, j].wait_recv()
+            for p in range(len(pieces)):
+                mix_copies[f, j, p].wait_recv()
         rows = mixed[f].reshape(row, width).astype(jnp.float32)
         attn_in = modulated(rows, mod[0], mod[1])
         if position == 0:
@@ -155,25 +169,26 @@
         heads_out = heads[...].T.astype(jnp.bfloat16)
         if position == 0:
             weights[1].wait()
-        for start, size in chunks(width, 384):
+        for p, (start, size) in enumerate(spans):
             part[f, :, start : start + size] = dot(
                 heads_out, out_w[:, start : start + size]
             ).astype(jnp.bfloat16)
-        for j, peer in enumerate(peers):
-            part_copies[f, j] = pltpu.make_async_remote_copy(
-                src_ref=part.at[f],
-                dst_ref=part_in.at[f, j],
-                send_sem=part_send.at[f, j],
-                recv_sem=part_recv.at[f, j],
-                device_id={"space": peer},
-                device_id_type=MESH,
-            )
-            part_copies[f, j].start()
+            for j, peer in enumerate(peers):
+                part_copies[f, j, p] = pltpu.make_async_remote_copy(
+                    src_ref=part.at[f, :, pl.ds(start, size)],
+                    dst_ref=part_in.at[f, j, :, pl.ds(start, size)],
+                    send_sem=part_send.at[f, j, p],
+                    recv_sem=part_recv.at[f, j, p],
+                    device_id={"space": peer},
+                    device_id_type=MESH,
+                )
+                part_copies[f, j, p].start()
 
     term_copies = {}
     for position, f in enumerate(order):
         for j in range(len(peers)):
-            part_copies[f, j].wait_recv()
+            for p in range(len(spans)):
+                part_copies[f, j, p].wait_recv()
         attn_sum = part[f].astype(jnp.float32)
         for j in range(len(peers)):
             attn_sum = attn_sum + part_in[f, j].astype(jnp.float32)
@@ -188,45 +203,49 @@
             ).astype(jnp.bfloat16)
         if position == 0:
             weights[3].wait()
-        for start, size in chunks(width, 384):
+        for p, (start, size) in enumerate(spans):
             term[f, :, :, start : start + size] = (
                 dot(active[...], down_w[:, start : start + size])
                 .astype(jnp.bfloat16)
                 .reshape(n_space, tokens, size)
             )
-        for j, peer in enumerate(peers):
-            term_copies[f, j] = pltpu.make_async_remote_copy(
-                src_ref=term.at[f, peer],
-                dst_ref=term_in.at[f, j],
-                send_sem=term_send.at[f, j],
-                recv_sem=term_recv.at[f, j],
-                device_id={"space": peer},
+            for j, peer in enumerate(peers):
+                term_copies[f, j, p] = pltpu.make_async_remote_copy(
+                    src_ref=term.at[f, peer, :, pl.ds(start, size)],
+                    dst_ref=term_in.at[f, j, :, pl.ds(start, size)],
+                    send_sem=term_send.at[f, j, p],
+                    recv_sem=term_recv.at[f, j, p],
+                    device_id={"space": peer},
+                    device_id_type=MESH,
+                )
+                term_copies[f, j, p].start()
+
+    end_copies = []
+    for f in order:
+        for p, (start, size) in enumerate(spans):
+            span = slice(start, start + size)
+            for j in range(len(peers)):
+                term_copies[f, j, p].wait_recv()
+            mlp_sum = term[f, me, :, span].astype(jnp.float32)
+            for j in range(len(peers)):
+                mlp_sum = mlp_sum + term_in[f, j, :, span].astype(jnp.float32)
+            final[f, :, span] = (hidden[f, me, :, span] + mod[5, :, span] * mlp_sum).astype(
+                jnp.bfloat16
+            )
+            copy = pltpu.make_async_remote_copy(
+                src_ref=final.at[f, :, pl.ds(start, size)],
+                dst_ref=result.at[0, f, :, pl.ds(start, size)],
+                send_sem=end_send.at[f, p],
+                recv_sem=end_recv.at[f, p],
+                device_id={"section": after},
                 device_id_type=MESH,
             )
-            term_copies[f, j].start()
-
-    end_copies = []
-    for f in order:
-        for j in range(len(peers)):
-            term_copies[f, j].wait_recv()
-        mlp_sum = term[f, me].astype(jnp.float32)
-        for j in range(len(peers)):
-            mlp_sum = mlp_sum + term_in[f, j].astype(jnp.float32)
-        final[f] = (hidden[f, me] + mod[5] * mlp_sum).astype(jnp.bfloat16)
-        copy = pltpu.make_async_remote_copy(
-            src_ref=final.at[f],
-            dst_ref=result.at[0, f],
-            send_sem=end_send.at[f],
-            recv_sem=end_recv.at[f],
-            device_id={"section": after},
-            device_id_type=MESH,
-        )
-        copy.start()
-        end_copies.append(copy)
+            copy.start()
+            end_copies.append(copy)
 
     @pl.when(tm < n_tm - 1)
     def _():
-        for copy in halo_copies:
+        for copy in halo_copies.values():
             copy.wait_send()
 
     for group in (mix_copies, part_copies, term_copies):
@@ -248,6 +267,7 @@
     anywhere = pl.BlockSpec(memory_space=pl.ANY)
     vmem = pl.BlockSpec(memory_space=pltpu.VMEM)
     total = n_frames * row
+    n_pieces, n_spans = len(row_pieces(tokens)), len(chunks(width, SPAN))
     return pl.pallas_call(
         functools.partial(layer, sizes),
         out_shape=jax.ShapeDtypeStruct(video.shape, bf16),
@@ -270,16 +290,16 @@
             pltpu.VMEM((width, units), bf16),
             pltpu.VMEM((units, width), bf16),
             sem((5,)),
-            sem((2,)),
-            sem((2,)),
-            sem((n_frames, others)),
-            sem((n_frames, others)),
-            sem((n_frames, others)),
-            sem((n_frames, others)),
-            sem((n_frames, others)),
-            sem((n_frames, others)),
-            sem((n_frames,)),
-            sem((n_frames,)),
+            sem((2, n_pieces)),
+            sem((2, n_pieces)),
+            sem((n_frames, others, n_pieces)),
+            sem((n_frames, others, n_pieces)),
+            sem((n_frames, others, n_spans)),
+            sem((n_frames, others, n_spans)),
+            sem((n_frames, others, n_spans)),
+            sem((n_frames, others, n_spans)),
+            sem((n_frames, n_spans)),
+            sem((n_frames, n_spans)),
         ],
         compiler_params=pltpu.CompilerParams(
             collective_id=0, has_side_effects=True, vmem_limit_bytes=56 * 1024 * 1024

time: 42.5 us -> 39.1 us (0.920)
  the two profiles are of different devices: /device:TPU:19 before, /device:TPU:17 now
where the time goes in v2:
time: 39.1 us; the launch traced here: 38.8 us
  Pallas kernels  37.1 us (95%)
  local copies, waits for them, and re-layouts  1.7 us (4%)
    pallas_call x1, Pallas kernels, body(): pl.pallas_call(functools.partial(layer, sizes), out_shape=jax.ShapeDtypeS...  37.1 us
    unnamed x1, local copies, waits for them, and re-layouts  1.7 us

profile of v2, /device:TPU:17, one launch (start us, length us, event | category | flops | bytes accessed | tf_op | source)
XLA Modules:
  0.0 38.8 jit_solution(45368964603897291)
XLA Ops:
  0.0 37.1 %shard_map.73 = bf16[1,2,64,1152]{3,2,1,0:T(8,128)(2,1)} custom-call(bf16[1,2,64,1152]{3,2,1,0:T(8,128)(2,1)} %video.1, f32[3,1,1152]{2,1,0:T(1,128)} %bitcast.5, f32[6,1,1152]{2,1,0:T(1,128)} %bitcast.4, bf16[1,3,576,1152]{3,2,1,0:T(8,128)(2,1)} %bitcast.3, bf16[1,576,1152]{2,1,0:T(8,128)(2,1)} %out_hbm.1, bf16[1,1152,2304]{2,1,0:T(8,128)(2,1)} %up_hbm.1, ...), custom_call_target="tpu_custom_call" | custom-call | flops 4076863488 | bytes 15925248 | tf_op jit(solution)/shard_map/pallas_call | solution.py:271
  37.1 1.7 %copy.9 = bf16[1,2,64,1152]{3,2,1,0:T(8,128)(2,1)} copy(bf16[1,2,64,1152]{3,2,1,0:T(8,128)(2,1)} %shard_map.73) | data formatting | bytes 589824
